TPU v7x, 32 devices: a whole 2x2x4 slice. The times are simulated.
32 devices in a mesh: groups: 2 (over x), gz: 16 (over z, y, core).
Axes of the slice: x: 2, y: 2, z: 4, core: 2. Of those that a mesh axis runs over, the one named last changes fastest.
Arguments:
- source: float32 [6, 32, 16384], P('groups', 'gz'), parts along dimension 0, may hold values from -6 to 6
- warm_start: float32 [6, 32, 16384], P('groups', 'gz'), parts along dimension 0, may hold values from -3 to 3
- coefficient: float32 [64, 16384], P(('groups', 'gz')), parts along dimension 0, may hold values from 0.1 to 10
Outputs:
- velocity: float32 [6, 32, 16384], P('groups', 'gz'), parts along dimension 0
There are 2 independent parts, one for each index of `groups`. A program takes and returns all parts, laid end to end along the dimension named above; each array names one. Nothing has to cross between parts.
All inputs are finite; a program needn't handle non-finite values.
Results may differ from a plain program's by a relative error of at most 0.00002.
Values sent between devices are 32-bit elements; how exact they have to be, the bound alone decides.
A program may use at most 64 MiB of HBM per device.

v0:
```python
import functools

import jax
import jax.numpy as jnp
from jax import lax
from jax.experimental import pallas as pl
from jax.experimental.pallas import tpu as pltpu
from jax.sharding import PartitionSpec as P

NY = 8
NX = 2048
NC = 4
OMEGA = 0.8
KEEP = 1.0 - OMEGA
TILES = NX // 128
QUARTER = TILES // 4
COMPS = 3

ID_COEF = 0
ID_CCOEF = 1
ID_FIELD = 2
ID_FLUX = ID_FIELD + 4 * COMPS
ID_CORR = ID_FLUX + COMPS
N_IDS = ID_CORR + NC * COMPS


def iotas(shape):
    row = lax.broadcasted_iota(jnp.int32, shape, len(shape) - 2)
    lane = lax.broadcasted_iota(jnp.int32, shape, len(shape) - 1)
    return row, lane


def roll_row(v, shift):
    return pltpu.roll(v, shift % 8, axis=v.ndim - 2)


def roll_lane(v, shift):
    return pltpu.roll(v, shift % 128, axis=v.ndim - 1)


def east_of(v):
    _, lane = iotas(v.shape)
    rolled = roll_lane(v, -1)
    after = jnp.concatenate([rolled[1:], rolled[:1]], axis=0)
    return jnp.where(lane == 127, after, rolled)


def west_of(v):
    _, lane = iotas(v.shape)
    rolled = roll_lane(v, 1)
    before = jnp.concatenate([rolled[-1:], rolled[:-1]], axis=0)
    return jnp.where(lane == 0, before, rolled)


def coarse_east_of(v):
    row, lane = iotas(v.shape[1:])
    rolled = roll_lane(v, -2)
    base = rolled[0]
    up = roll_row(base, -1)
    down = roll_lane(roll_row(base, 1), -1)
    last = jnp.where(row % 2 == 0, up, down)
    after = jnp.concatenate([rolled[1:], last[None]], axis=0)
    return jnp.where((lane >= 126)[None], after, rolled)


def coarse_west_of(v):
    row, lane = iotas(v.shape[1:])
    rolled = roll_lane(v, 2)
    base = rolled[-1]
    up = roll_lane(roll_row(base, -1), 1)
    down = roll_row(base, 1)
    up = jnp.where(lane == 0, 0.0, up)
    first = jnp.where(row % 2 == 0, up, down)
    before = jnp.concatenate([first[None], rolled[:-1]], axis=0)
    return jnp.where((lane < 2)[None], before, rolled)


def block_sum(v):
    row, lane = iotas((QUARTER, 8, 128))
    even_row, even_lane = (row % 2 == 0, lane % 2 == 0)
    q = [v[i * QUARTER:(i + 1) * QUARTER] for i in range(4)]

    def rows(a, b):
        x = jnp.where(even_row, a, b)
        y = jnp.where(even_row, b, a)
        return x + jnp.where(even_row, roll_row(y, -1), roll_row(y, 1))

    a, b = rows(q[0], q[1]), rows(q[2], q[3])
    x = jnp.where(even_lane, a, b)
    y = jnp.where(even_lane, b, a)
    return x + jnp.where(even_lane, roll_lane(y, -1), roll_lane(y, 1))


def widen(v):
    row, lane = iotas(v.shape)
    even_row, even_lane = (row % 2 == 0, lane % 2 == 0)
    e = jnp.where(even_row, v, roll_row(v, 1))
    o = jnp.where(even_row, roll_row(v, -1), v)
    return jnp.concatenate(
        [
            jnp.where(even_lane, e, roll_lane(e, 1)),
            jnp.where(even_lane, o, roll_lane(o, 1)),
            jnp.where(even_lane, roll_lane(e, -1), e),
            jnp.where(even_lane, roll_lane(o, -1), o),
        ],
        axis=0,
    )


def kernel(
    src_hbm, warm_hbm, coef_hbm, out_hbm,
    src_raw, warm_raw, coef_raw, out_raw,
    src, field, halo, coef, coef_halo, face_e, face_n, face_m, face_z, gain,
    ccoef, ccoef_halo, cface_e, cface_n, cface_z, cgain,
    flux, flux_halo, rhs, corr, corr_halo,
    in_sem, out_sem, send_sem, recv_sem,
):
    me = lax.axis_index("gz")
    count = lax.axis_size("gz")
    has_lo, has_up = me > 0, me < count - 1
    has = (has_lo, has_up)
    other = (me - 1, me + 1)
    comp_rows = 2 * NY * TILES

    def comp_slice(c):
        return pl.ds(c * comp_rows, comp_rows)

    coef_in = pltpu.make_async_copy(coef_hbm, coef_raw, in_sem.at[0])
    warm_in = [
        pltpu.make_async_copy(
            warm_hbm.at[comp_slice(c)], warm_raw.at[comp_slice(c)], in_sem.at[1 + c])
        for c in range(COMPS)
    ]
    src_in = [
        pltpu.make_async_copy(
            src_hbm.at[comp_slice(c)], src_raw.at[comp_slice(c)], in_sem.at[1 + COMPS + c])
        for c in range(COMPS)
    ]
    barrier = pltpu.get_barrier_semaphore()
    for d in range(2):
        @pl.when(has[d])
        def _():
            pl.semaphore_signal(
                barrier, inc=1, device_id={"gz": other[d]},
                device_id_type=pl.DeviceIdType.MESH)
    coef_in.start()
    for c in range(COMPS):
        warm_in[c].start()
    for c in range(COMPS):
        src_in[c].start()

    def copy(key, d, source, target):
        return pltpu.make_async_remote_copy(
            src_ref=source, dst_ref=target.at[1 - d],
            send_sem=send_sem.at[key, d], recv_sem=recv_sem.at[key, 1 - d],
            device_id={"gz": other[d]}, device_id_type=pl.DeviceIdType.MESH)

    sent = []

    def send(key, sources, target):
        for d in range(2):
            @pl.when(has[d])
            def _():
                copy(key, d, sources[d], target).start()
        sent.append((key, sources, target))

    def arrive(key, sources, target):
        for d in range(2):
            @pl.when(has[1 - d])
            def _():
                copy(key, d, sources[d], target).wait_recv()

    for d in range(2):
        @pl.when(jnp.logical_not(has[d]))
        def _():
            for t in range(4):
                for c in range(COMPS):
                    halo[t, c, d] = jnp.zeros((TILES, 8, 128), jnp.float32)
            coef_halo[d] = jnp.zeros((TILES, 8, 128), jnp.float32)
            ccoef_halo[d] = jnp.zeros((QUARTER, 8, 128), jnp.float32)
            for c in range(COMPS):
                flux_halo[c, d] = jnp.zeros((QUARTER, 8, 128), jnp.float32)
            for r in range(NC):
                for c in range(COMPS):
                    corr_halo[r, c, d] = jnp.zeros((QUARTER, 8, 128), jnp.float32)

    def spread(raw, first, target):
        for p in range(2):
            for x in range(TILES):
                target[p, x] = raw[pl.ds(first + 2 * x + p, NY, stride=2 * TILES), :]

    coef_in.wait()
    spread(coef_raw, 0, coef)
    warm_in[0].wait()
    spread(warm_raw, 0, field.at[0, 0])
    pl.semaphore_wait(barrier, has_lo.astype(jnp.int32) + has_up.astype(jnp.int32))

    def field_args(t, c):
        return (ID_FIELD + COMPS * t + c,
                (field.at[t, c, 0], field.at[t, c, 1]), halo.at[t, c])

    coef_args = (ID_COEF, (coef.at[0], coef.at[1]), coef_halo)
    send(*coef_args)
    send(*field_args(0, 0))
    for c in range(1, COMPS):
        warm_in[c].wait()
        spread(warm_raw, c * comp_rows, field.at[0, c])
        send(*field_args(0, c))
    ccoef[...] = 0.125 * block_sum(coef[0] + coef[1])
    ccoef_args = (ID_CCOEF, (ccoef, ccoef), ccoef_halo)
    send(*ccoef_args)

    shape = (TILES, 8, 128)
    tile = lax.broadcasted_iota(jnp.int32, shape, 0)
    row, lane = iotas(shape)
    last_column = (tile == TILES - 1) & (lane == 127)
    for p in range(2):
        a = coef[p]
        face_e[p] = jnp.where(last_column, 0.0, 0.5 * (a + east_of(a)))
        face_n[p] = jnp.where(row == NY - 1, 0.0, 0.5 * (a + roll_row(a, -1)))
    face_m[...] = 0.5 * (coef[0] + coef[1])
    for c in range(COMPS):
        src_in[c].wait()
        spread(src_raw, c * comp_rows, src.at[c])
    arrive(*coef_args)
    for p in range(2):
        z = jnp.where(has[p], 0.5 * (coef[p] + coef_halo[p]), 0.0)
        face_z[p] = z
        e, n = face_e[p], face_n[p]
        total = e + west_of(e) + n + roll_row(n, 1) + z + face_m[...]
        gain[p] = OMEGA / (1.0 + total)

    def pulled(u, p, u_other, u_halo):
        e, n = face_e[p], face_n[p]
        out = e * east_of(u) + west_of(e * u)
        out = out + n * roll_row(u, -1) + roll_row(n * u, 1)
        out = out + face_m[...] * u_other
        if u_halo is not None:
            out = out + face_z[p] * u_halo
        return out

    def sweep(u, c, u_halo):
        return [
            KEEP * u[p] + gain[p] * (src[c, p] + pulled(u[p], p, u[1 - p], u_halo[p]))
            for p in range(2)
        ]

    def flux_args(c):
        return (ID_FLUX + c, (flux.at[c, 0], flux.at[c, 1]), flux_halo.at[c])

    def corr_args(r, c):
        return (ID_CORR + COMPS * r + c, (corr.at[r, c], corr.at[r, c]), corr_halo.at[r, c])

    for c in range(COMPS):
        arrive(*field_args(0, c))
        new = sweep([field[0, c, p] for p in range(2)], c, [halo[0, c, p] for p in range(2)])
        for p in range(2):
            field[1, c, p] = new[p]
        send(*field_args(1, c))

    cshape = (QUARTER, 8, 128)
    ctile = lax.broadcasted_iota(jnp.int32, cshape, 0)
    crow, clane = iotas(cshape)
    clast = (ctile == QUARTER - 1) & (clane == 127) & (crow % 2 == 1)
    a = ccoef[...]
    e = jnp.where(clast, 0.0, 0.125 * (a + coarse_east_of(a)))
    n = jnp.where(crow >= NY - 2, 0.0, 0.125 * (a + roll_row(a, -2)))
    cface_e[...] = e
    cface_n[...] = n
    total = e + coarse_west_of(e) + n + roll_row(n, 2)
    arrive(*ccoef_args)
    for d in range(2):
        z = jnp.where(has[d], 0.125 * (a + ccoef_halo[d]), 0.0)
        cface_z[d] = z
        total = total + z
    cgain[...] = OMEGA / (1.0 + total)

    for c in range(COMPS):
        arrive(*field_args(1, c))
        new = sweep([field[1, c, p] for p in range(2)], c, [halo[1, c, p] for p in range(2)])
        for p in range(2):
            field[2, c, p] = new[p]
            flux[c, p] = block_sum(face_z[p] * new[p])
        send(*flux_args(c))

    for c in range(COMPS):
        u = [field[2, c, p] for p in range(2)]
        res = [
            src[c, p] + pulled(u[p], p, u[1 - p], None) - (OMEGA / gain[p]) * u[p]
            for p in range(2)
        ]
        rhs[c] = block_sum(res[0] + res[1])

    for c in range(COMPS):
        arrive(*flux_args(c))
        r = 0.125 * (rhs[c] + flux_halo[c, 0] + flux_halo[c, 1])
        rhs[c] = r
        corr[0, c] = cgain[...] * r
        send(*corr_args(0, c))

    for r in range(1, NC):
        send(*field_args(2, r - 1))
        for c in range(COMPS):
            u = corr[r - 1, c]
            e, n = cface_e[...], cface_n[...]
            out = e * coarse_east_of(u) + coarse_west_of(e * u)
            out = out + n * roll_row(u, -2) + roll_row(n * u, 2)
            arrive(*corr_args(r - 1, c))
            out = out + cface_z[0] * corr_halo[r - 1, c, 0] + cface_z[1] * corr_halo[r - 1, c, 1]
            corr[r, c] = KEEP * u + cgain[...] * (rhs[c] + out)
            send(*corr_args(r, c))

    for c in range(COMPS):
        add = widen(corr[NC - 1, c])
        u = [field[2, c, p] + add for p in range(2)]
        arrive(*field_args(2, c))
        arrive(*corr_args(NC - 1, c))
        u_halo = [halo[2, c, d] + widen(corr_halo[NC - 1, c, d]) for d in range(2)]
        new = sweep(u, c, u_halo)
        for p in range(2):
            field[3, c, p] = new[p]
        send(*field_args(3, c))

    outs = []
    for c in range(COMPS):
        arrive(*field_args(3, c))
        new = sweep([field[3, c, p] for p in range(2)], c, [halo[3, c, p] for p in range(2)])
        for p in range(2):
            for x in range(TILES):
                out_raw[pl.ds(c * comp_rows + 2 * x + p, NY, stride=2 * TILES), :] = new[p][x]
        done = pltpu.make_async_copy(
            out_raw.at[comp_slice(c)], out_hbm.at[comp_slice(c)], out_sem.at[c])
        done.start()
        outs.append(done)
    for key, sources, target in sent:
        for d in range(2):
            @pl.when(has[d])
            def _():
                copy(key, d, sources[d], target).wait_send()
    for done in outs:
        done.wait()


def body(source, warm_start, coefficient):
    comps, planes, cells = source.shape
    rows = planes * cells // 128

    def flat(array):
        lead = array.shape[:-2]
        split = array.reshape(lead + (planes, cells // 128, 128))
        return jnp.swapaxes(split, -3, -2).reshape(-1, 128)

    def vm(*shape):
        return pltpu.VMEM(shape + (8, 128), jnp.float32)

    raw = pltpu.VMEM((comps * rows, 128), jnp.float32)
    out = pl.pallas_call(
        kernel,
        out_shape=jax.ShapeDtypeStruct((comps * rows, 128), jnp.float32),
        in_specs=[pl.BlockSpec(memory_space=pl.ANY)] * 3,
        out_specs=pl.BlockSpec(memory_space=pl.ANY),
        scratch_shapes=[
            raw, raw, pltpu.VMEM((rows, 128), jnp.float32), raw,
            vm(comps, 2, TILES),
            vm(4, comps, 2, TILES),
            vm(4, comps, 2, TILES),
            vm(2, TILES), vm(2, TILES),
            vm(2, TILES), vm(2, TILES), vm(TILES), vm(2, TILES), vm(2, TILES),
            vm(QUARTER), vm(2, QUARTER),
            vm(QUARTER), vm(QUARTER), vm(2, QUARTER), vm(QUARTER),
            vm(comps, 2, QUARTER), vm(comps, 2, QUARTER),
            vm(comps, QUARTER),
            vm(NC, comps, QUARTER), vm(NC, comps, 2, QUARTER),
            pltpu.SemaphoreType.DMA((1 + 2 * COMPS,)),
            pltpu.SemaphoreType.DMA((COMPS,)),
            pltpu.SemaphoreType.DMA((N_IDS, 2)),
            pltpu.SemaphoreType.DMA((N_IDS, 2)),
        ],
        compiler_params=pltpu.CompilerParams(
            collective_id=0, has_side_effects=True, vmem_limit_bytes=48 * 1024 * 1024),
    )(flat(source), flat(warm_start), flat(coefficient))
    out = out.reshape(comps, cells // 128, planes, 128)
    return jnp.swapaxes(out, 1, 2).reshape(comps, planes, cells)


def solution(mesh):
    in_specs = (P("groups", "gz", None), P("groups", "gz", None), P(("groups", "gz"), None))
    out_specs = P("groups", "gz", None)
    return jax.shard_map(body, mesh=mesh, in_specs=in_specs, out_specs=out_specs, check_vma=False)
```

profile of v0, /device:TPU:20, one launch (start us, length us, event | category | flops | bytes accessed | tf_op | source)
XLA Modules:
  0.0 37.9 jit_solution(10461239865866909340)
XLA Ops:
  0.0 0.0 copy-start
  0.0 1.0 %copy-done = f32[3,2,16384]{2,1,0:T(2,128)S(1)} copy-done((f32[3,2,16384]{2,1,0:T(2,128)S(1)}, f32[3,2,16384]{2,1,0:T(2,128)}, u32[]{:S(2)}) %copy-start) | copy-done | bytes 393240
  1.0 0.0 copy-start.1
  1.0 1.0 %copy-done.1 = f32[3,2,16384]{2,1,0:T(2,128)S(1)} copy-done((f32[3,2,16384]{2,1,0:T(2,128)S(1)}, f32[3,2,16384]{2,1,0:T(2,128)}, u32[]{:S(2)}) %copy-start.1) | copy-done | bytes 393240
  2.0 0.0 copy-start.2
  2.0 0.9 %copy-done.2 = f32[2,16384]{1,0:T(2,128)S(1)} copy-done((f32[2,16384]{1,0:T(2,128)S(1)}, f32[2,16384]{1,0:T(2,128)}, u32[]{:S(2)}) %copy-start.2) | copy-done | bytes 131096
  2.9 34.2 %shard_map.37 = f32[768,128]{1,0:T(8,128)S(1)} custom-call(f32[768,128]{1,0:T(8,128)S(1)} %bitcast.21, f32[768,128]{1,0:T(8,128)S(1)} %bitcast.22, f32[256,128]{1,0:T(8,128)S(1)} %bitcast.23), custom_call_target="tpu_custom_call" | custom-call | tf_op jit(solution)/shard_map/pallas_call | solution.py:357
  37.1 0.7 %copy.9 = f32[3,2,16384]{2,1,0:T(2,128)} copy(f32[3,2,16384]{2,1,0:T(2,128)S(1)} %bitcast.20) | data formatting | bytes 786432
Async XLA Ops:
  0.0 1.0 %copy-start = (f32[3,2,16384]{2,1,0:T(2,128)S(1)}, f32[3,2,16384]{2,1,0:T(2,128)}, u32[]{:S(2)}) copy-start(f32[3,2,16384]{2,1,0:T(2,128)} %param.3) | copy-start | bytes 1179652
  1.0 1.0 %copy-start.1 = (f32[3,2,16384]{2,1,0:T(2,128)S(1)}, f32[3,2,16384]{2,1,0:T(2,128)}, u32[]{:S(2)}) copy-start(f32[3,2,16384]{2,1,0:T(2,128)} %param.4) | copy-start | bytes 1179652
  2.0 0.9 %copy-start.2 = (f32[2,16384]{1,0:T(2,128)S(1)}, f32[2,16384]{1,0:T(2,128)}, u32[]{:S(2)}) copy-start(f32[2,16384]{1,0:T(2,128)} %param.5) | copy-start | bytes 393220
where the time goes:
time: 38.1 us; the launch traced here: 37.9 us
  Pallas kernels  34.2 us (90%)
  local copies, waits for them, and re-layouts  3.64 us (10%)
    pallas_call x1, Pallas kernels, body(): pl.pallas_call(kernel, out_shape=jax.ShapeDtypeStruct((comps * rows, 128)...  34.2 us
    unnamed x7, local copies, waits for them, and re-layouts  3.64 us

commit v1 on v0

--- a/solution.py
+++ b/solution.py
@@ -15,11 +15,14 @@
 TILES = NX // 128
 QUARTER = TILES // 4
 COMPS = 3
+PIECES = 2
+PIECE = TILES // PIECES
+SLOTS = (2, 1, 1, 1, 1)
 
 ID_COEF = 0
 ID_CCOEF = 1
 ID_FIELD = 2
-ID_FLUX = ID_FIELD + 4 * COMPS
+ID_FLUX = ID_FIELD + 4 * COMPS * PIECES
 ID_CORR = ID_FLUX + COMPS
 N_IDS = ID_CORR + NC * COMPS
 
@@ -175,14 +178,14 @@
         def _():
             for t in range(4):
                 for c in range(COMPS):
-                    halo[t, c, d] = jnp.zeros((TILES, 8, 128), jnp.float32)
+                    halo[t, d, c] = jnp.zeros((TILES, 8, 128), jnp.float32)
             coef_halo[d] = jnp.zeros((TILES, 8, 128), jnp.float32)
             ccoef_halo[d] = jnp.zeros((QUARTER, 8, 128), jnp.float32)
             for c in range(COMPS):
                 flux_halo[c, d] = jnp.zeros((QUARTER, 8, 128), jnp.float32)
             for r in range(NC):
                 for c in range(COMPS):
-                    corr_halo[r, c, d] = jnp.zeros((QUARTER, 8, 128), jnp.float32)
+                    corr_halo[r, d, c] = jnp.zeros((QUARTER, 8, 128), jnp.float32)
 
     def spread(raw, first, target):
         for p in range(2):
@@ -195,20 +198,31 @@
     spread(warm_raw, 0, field.at[0, 0])
     pl.semaphore_wait(barrier, has_lo.astype(jnp.int32) + has_up.astype(jnp.int32))
 
-    def field_args(t, c):
-        return (ID_FIELD + COMPS * t + c,
-                (field.at[t, c, 0], field.at[t, c, 1]), halo.at[t, c])
+    def field_args(t, c, h):
+        tiles = pl.ds(h * PIECE, PIECE)
+        return (ID_FIELD + (COMPS * t + c) * PIECES + h,
+                (field.at[t, c, 0, tiles], field.at[t, c, 1, tiles]), halo.at[t, :, c, tiles])
+
+    def send_field(t, c):
+        for h in range(PIECES):
+            send(*field_args(t, c, h))
+
+    smoothed = [(c, h) for c in range(COMPS) for h in range(PIECES)]
+
+    def send_smoothed(slot):
+        first = sum(SLOTS[:slot])
+        for c, h in smoothed[first:first + SLOTS[slot]]:
+            send(*field_args(2, c, h))
 
     coef_args = (ID_COEF, (coef.at[0], coef.at[1]), coef_halo)
     send(*coef_args)
-    send(*field_args(0, 0))
+    send_field(0, 0)
     for c in range(1, COMPS):
         warm_in[c].wait()
         spread(warm_raw, c * comp_rows, field.at[0, c])
-        send(*field_args(0, c))
+        send_field(0, c)
     ccoef[...] = 0.125 * block_sum(coef[0] + coef[1])
     ccoef_args = (ID_CCOEF, (ccoef, ccoef), ccoef_halo)
-    send(*ccoef_args)
 
     shape = (TILES, 8, 128)
     tile = lax.broadcasted_iota(jnp.int32, shape, 0)
@@ -230,33 +244,58 @@
         total = e + west_of(e) + n + roll_row(n, 1) + z + face_m[...]
         gain[p] = OMEGA / (1.0 + total)
 
-    def pulled(u, p, u_other, u_halo):
+    def pulled(u, p):
         e, n = face_e[p], face_n[p]
-        out = e * east_of(u) + west_of(e * u)
-        out = out + n * roll_row(u, -1) + roll_row(n * u, 1)
-        out = out + face_m[...] * u_other
-        if u_halo is not None:
-            out = out + face_z[p] * u_halo
-        return out
-
-    def sweep(u, c, u_halo):
-        return [
-            KEEP * u[p] + gain[p] * (src[c, p] + pulled(u[p], p, u[1 - p], u_halo[p]))
+        out = e * east_of(u[p]) + west_of(e * u[p])
+        out = out + n * roll_row(u[p], -1) + roll_row(n * u[p], 1)
+        return out + face_m[...] * u[1 - p]
+
+    def sweep_own(u, c):
+        return [KEEP * u[p] + gain[p] * (src[c, p] + pulled(u, p)) for p in range(2)]
+
+    def sweep_rest(own, t, c, h, wide):
+        tiles = slice(h * PIECE, (h + 1) * PIECE)
+        new = []
+        for p in range(2):
+            u_halo = halo[t, p, c, tiles]
+            if wide is not None:
+                u_halo = u_halo + wide[p][tiles]
+            new.append(own[p][tiles] + gain[p, tiles] * (face_z[p, tiles] * u_halo))
+        return new
+
+    def next_field(t, c, own, wide=None):
+        for h in range(PIECES):
+            arrive(*field_args(t, c, h))
+            new = sweep_rest(own, t, c, h, wide)
+            for p in range(2):
+                field[t + 1, c, p, h * PIECE:(h + 1) * PIECE] = new[p]
+            if t != 1:
+                send(*field_args(t + 1, c, h))
+
+    def flux_args(c):
+        return (ID_FLUX + c, (flux.at[c, 0], flux.at[c, 1]), flux_halo.at[c])
+
+    def corr_args(r, c):
+        return (ID_CORR + COMPS * r + c, (corr.at[r, c], corr.at[r, c]), corr_halo.at[r, :, c])
+
+    for c in range(COMPS):
+        next_field(0, c, sweep_own([field[0, c, p] for p in range(2)], c))
+    send(*ccoef_args)
+
+    for c in range(COMPS):
+        next_field(1, c, sweep_own([field[1, c, p] for p in range(2)], c))
+        for p in range(2):
+            flux[c, p] = block_sum(face_z[p] * field[2, c, p])
+        send(*flux_args(c))
+
+    send_smoothed(0)
+    for c in range(COMPS):
+        u = [field[2, c, p] for p in range(2)]
+        res = [
+            src[c, p] + pulled(u, p) - (OMEGA / gain[p]) * u[p]
             for p in range(2)
         ]
-
-    def flux_args(c):
-        return (ID_FLUX + c, (flux.at[c, 0], flux.at[c, 1]), flux_halo.at[c])
-
-    def corr_args(r, c):
-        return (ID_CORR + COMPS * r + c, (corr.at[r, c], corr.at[r, c]), corr_halo.at[r, c])
-
-    for c in range(COMPS):
-        arrive(*field_args(0, c))
-        new = sweep([field[0, c, p] for p in range(2)], c, [halo[0, c, p] for p in range(2)])
-        for p in range(2):
-            field[1, c, p] = new[p]
-        send(*field_args(1, c))
+        rhs[c] = block_sum(res[0] + res[1])
 
     cshape = (QUARTER, 8, 128)
     ctile = lax.broadcasted_iota(jnp.int32, cshape, 0)
@@ -276,22 +315,6 @@
     cgain[...] = OMEGA / (1.0 + total)
 
     for c in range(COMPS):
-        arrive(*field_args(1, c))
-        new = sweep([field[1, c, p] for p in range(2)], c, [halo[1, c, p] for p in range(2)])
-        for p in range(2):
-            field[2, c, p] = new[p]
-            flux[c, p] = block_sum(face_z[p] * new[p])
-        send(*flux_args(c))
-
-    for c in range(COMPS):
-        u = [field[2, c, p] for p in range(2)]
-        res = [
-            src[c, p] + pulled(u[p], p, u[1 - p], None) - (OMEGA / gain[p]) * u[p]
-            for p in range(2)
-        ]
-        rhs[c] = block_sum(res[0] + res[1])
-
-    for c in range(COMPS):
         arrive(*flux_args(c))
         r = 0.125 * (rhs[c] + flux_halo[c, 0] + flux_halo[c, 1])
         rhs[c] = r
@@ -299,35 +322,37 @@
         send(*corr_args(0, c))
 
     for r in range(1, NC):
-        send(*field_args(2, r - 1))
+        send_smoothed(r)
+        own = []
         for c in range(COMPS):
             u = corr[r - 1, c]
             e, n = cface_e[...], cface_n[...]
             out = e * coarse_east_of(u) + coarse_west_of(e * u)
             out = out + n * roll_row(u, -2) + roll_row(n * u, 2)
+            own.append(KEEP * u + cgain[...] * (rhs[c] + out))
+        for c in range(COMPS):
             arrive(*corr_args(r - 1, c))
-            out = out + cface_z[0] * corr_halo[r - 1, c, 0] + cface_z[1] * corr_halo[r - 1, c, 1]
-            corr[r, c] = KEEP * u + cgain[...] * (rhs[c] + out)
+            out = cface_z[0] * corr_halo[r - 1, 0, c] + cface_z[1] * corr_halo[r - 1, 1, c]
+            corr[r, c] = own[c] + cgain[...] * out
             send(*corr_args(r, c))
 
+    send_smoothed(NC)
     for c in range(COMPS):
         add = widen(corr[NC - 1, c])
-        u = [field[2, c, p] + add for p in range(2)]
-        arrive(*field_args(2, c))
+        own = sweep_own([field[2, c, p] + add for p in range(2)], c)
         arrive(*corr_args(NC - 1, c))
-        u_halo = [halo[2, c, d] + widen(corr_halo[NC - 1, c, d]) for d in range(2)]
-        new = sweep(u, c, u_halo)
-        for p in range(2):
-            field[3, c, p] = new[p]
-        send(*field_args(3, c))
+        next_field(2, c, own, [widen(corr_halo[NC - 1, d, c]) for d in range(2)])
 
     outs = []
     for c in range(COMPS):
-        arrive(*field_args(3, c))
-        new = sweep([field[3, c, p] for p in range(2)], c, [halo[3, c, p] for p in range(2)])
-        for p in range(2):
-            for x in range(TILES):
-                out_raw[pl.ds(c * comp_rows + 2 * x + p, NY, stride=2 * TILES), :] = new[p][x]
+        own = sweep_own([field[3, c, p] for p in range(2)], c)
+        for h in range(PIECES):
+            arrive(*field_args(3, c, h))
+            new = sweep_rest(own, 3, c, h, None)
+            for p in range(2):
+                for x in range(PIECE):
+                    first = c * comp_rows + 2 * (h * PIECE + x) + p
+                    out_raw[pl.ds(first, NY, stride=2 * TILES), :] = new[p][x]
         done = pltpu.make_async_copy(
             out_raw.at[comp_slice(c)], out_hbm.at[comp_slice(c)], out_sem.at[c])
         done.start()
@@ -363,21 +388,21 @@
             raw, raw, pltpu.VMEM((rows, 128), jnp.float32), raw,
             vm(comps, 2, TILES),
             vm(4, comps, 2, TILES),
-            vm(4, comps, 2, TILES),
+            vm(4, 2, comps, TILES),
             vm(2, TILES), vm(2, TILES),
             vm(2, TILES), vm(2, TILES), vm(TILES), vm(2, TILES), vm(2, TILES),
             vm(QUARTER), vm(2, QUARTER),
             vm(QUARTER), vm(QUARTER), vm(2, QUARTER), vm(QUARTER),
             vm(comps, 2, QUARTER), vm(comps, 2, QUARTER),
             vm(comps, QUARTER),
-            vm(NC, comps, QUARTER), vm(NC, comps, 2, QUARTER),
+            vm(NC, comps, QUARTER), vm(NC, 2, comps, QUARTER),
             pltpu.SemaphoreType.DMA((1 + 2 * COMPS,)),
             pltpu.SemaphoreType.DMA((COMPS,)),
             pltpu.SemaphoreType.DMA((N_IDS, 2)),
             pltpu.SemaphoreType.DMA((N_IDS, 2)),
         ],
         compiler_params=pltpu.CompilerParams(
-            collective_id=0, has_side_effects=True, vmem_limit_bytes=48 * 1024 * 1024),
+            collective_id=0, has_side_effects=True, vmem_limit_bytes=54528 * 1024),
     )(flat(source), flat(warm_start), flat(coefficient))
     out = out.reshape(comps, cells // 128, planes, 128)
     return jnp.swapaxes(out, 1, 2).reshape(comps, planes, cells)

time: 38.1 us -> 35.9 us (0.942)
  local copies, waits for them, and re-layouts: 3.64 us -> 1.65 us
    unnamed x7 -> x3, local copies, waits for them, and re-layouts: 3.64 us -> 1.65 us
where the time goes in v1:
time: 35.9 us; the launch traced here: 35.8 us
  Pallas kernels  34.1 us (95%)
  local copies, waits for them, and re-layouts  1.65 us (5%)
    pallas_call x1, Pallas kernels, body(): pl.pallas_call(kernel, out_shape=jax.ShapeDtypeStruct((comps * rows, 128)...  34.1 us
    unnamed x3, local copies, waits for them, and re-layouts  1.65 us

profile of v1, /device:TPU:20, one launch (start us, length us, event | category | flops | bytes accessed | tf_op | source)
XLA Modules:
  0.0 35.8 jit_solution(4786259203123740265)
XLA Ops:
  0.0 0.0 copy-start
  0.0 0.9 %copy-done = f32[2,16384]{1,0:T(2,128)S(1)} copy-done((f32[2,16384]{1,0:T(2,128)S(1)}, f32[2,16384]{1,0:T(2,128)}, u32[]{:S(2)}) %copy-start) | copy-done | bytes 131096
  0.9 34.1 %shard_map.37 = f32[768,128]{1,0:T(8,128)S(1)} custom-call(f32[768,128]{1,0:T(8,128)} %bitcast.22, f32[768,128]{1,0:T(8,128)} %bitcast.23, f32[256,128]{1,0:T(8,128)S(1)} %bitcast.21), custom_call_target="tpu_custom_call" | custom-call | tf_op jit(solution)/shard_map/pallas_call | solution.py:382
  35.0 0.7 %copy.9 = f32[3,2,16384]{2,1,0:T(2,128)} copy(f32[3,2,16384]{2,1,0:T(2,128)S(1)} %bitcast.20) | data formatting | bytes 786432
Async XLA Ops:
  0.0 0.9 %copy-start = (f32[2,16384]{1,0:T(2,128)S(1)}, f32[2,16384]{1,0:T(2,128)}, u32[]{:S(2)}) copy-start(f32[2,16384]{1,0:T(2,128)} %param.5) | copy-start | bytes 393220

commit v2 on v1

--- a/solution.py
+++ b/solution.py
@@ -173,6 +173,14 @@
             def _():
                 copy(key, d, sources[d], target).wait_recv()
 
+    def drain(keep=0):
+        while len(sent) > keep:
+            key, sources, target = sent.pop(0)
+            for d in range(2):
+                @pl.when(has[d])
+                def _():
+                    copy(key, d, sources[d], target).wait_send()
+
     for d in range(2):
         @pl.when(jnp.logical_not(has[d]))
         def _():
@@ -343,6 +351,7 @@
         arrive(*corr_args(NC - 1, c))
         next_field(2, c, own, [widen(corr_halo[NC - 1, d, c]) for d in range(2)])
 
+    drain(COMPS * PIECES)
     outs = []
     for c in range(COMPS):
         own = sweep_own([field[3, c, p] for p in range(2)], c)
@@ -357,11 +366,7 @@
             out_raw.at[comp_slice(c)], out_hbm.at[comp_slice(c)], out_sem.at[c])
         done.start()
         outs.append(done)
-    for key, sources, target in sent:
-        for d in range(2):
-            @pl.when(has[d])
-            def _():
-                copy(key, d, sources[d], target).wait_send()
+    drain()
     for done in outs:
         done.wait()
 

time: 35.9 us -> 35.8 us (level)
  no operation moved by 1% of the time
where the time goes in v2:
time: 35.8 us; the launch traced here: 35.7 us
  Pallas kernels  34 us (95%)
  local copies, waits for them, and re-layouts  1.65 us (5%)
    pallas_call x1, Pallas kernels, body(): pl.pallas_call(kernel, out_shape=jax.ShapeDtypeStruct((comps * rows, 128)...  34 us
    unnamed x3, local copies, waits for them, and re-layouts  1.65 us

profile of v2, /device:TPU:20, one launch (start us, length us, event | category | flops | bytes accessed | tf_op | source)
XLA Modules:
  0.0 35.7 jit_solution(14628375207407205442)
XLA Ops:
  0.0 0.0 copy-start
  0.0 0.9 %copy-done = f32[2,16384]{1,0:T(2,128)S(1)} copy-done((f32[2,16384]{1,0:T(2,128)S(1)}, f32[2,16384]{1,0:T(2,128)}, u32[]{:S(2)}) %copy-start) | copy-done | bytes 131096
  0.9 34.0 %shard_map.37 = f32[768,128]{1,0:T(8,128)S(1)} custom-call(f32[768,128]{1,0:T(8,128)} %bitcast.22, f32[768,128]{1,0:T(8,128)} %bitcast.23, f32[256,128]{1,0:T(8,128)S(1)} %bitcast.21), custom_call_target="tpu_custom_call" | custom-call | tf_op jit(solution)/shard_map/pallas_call | solution.py:387
  34.9 0.7 %copy.9 = f32[3,2,16384]{2,1,0:T(2,128)} copy(f32[3,2,16384]{2,1,0:T(2,128)S(1)} %bitcast.20) | data formatting | bytes 786432
Async XLA Ops:
  0.0 0.9 %copy-start = (f32[2,16384]{1,0:T(2,128)S(1)}, f32[2,16384]{1,0:T(2,128)}, u32[]{:S(2)}) copy-start(f32[2,16384]{1,0:T(2,128)} %param.5) | copy-start | bytes 393220
